TPU v7x, 32 devices: a whole 2x2x4 slice. The times are simulated.
32 devices in a mesh: req: 8 (over z, x), tp: 4 (over y, core).
Axes of the slice: x: 2, y: 2, z: 4, core: 2. Of those that a mesh axis runs over, the one named last changes fastest.
Arguments:
- layer_in: bfloat16 [4, 64, 2880], P(None, 'req'), may hold values from -3 to 3
- query_in: bfloat16 [4, 64, 2048], P(None, 'req', 'tp'), may hold values from -6 to 6
- unrotated_key: bfloat16 [4, 64, 512], P(None, 'req', 'tp'), may hold values from -6 to 6
- incoming_value: bfloat16 [4, 64, 512], P(None, 'req', 'tp'), may hold values from -12 to 12
- rotated_prompt_keys: bfloat16 [64, 256, 512], P('req', None, 'tp'), may hold values from -270 to 270
- prompt_value_rows: bfloat16 [64, 256, 512], P('req', None, 'tp'), may hold values from -6 to 6
- generated_key_rows: bfloat16 [64, 64, 512], P('req', None, 'tp'), may hold values from -9 to 9
- generated_value_rows: bfloat16 [64, 64, 512], P('req', None, 'tp'), may hold values from -12 to 12
- lengths: int32 [8], replicated, may hold values from 128 to 2048, as said below
- parents: int32 [4, 8, 8], replicated, may hold values from 0 to 7
- routes: int32 [4, 64, 4], P(None, 'req'), may hold values from 0 to 15, all different within a row; in each aligned block of 8 rows (0 to 7, 8 to 15, ..., all dimensions but the last counted through in order) at most 4 rows name the same one
- head_sink_logits: float32 [32], P('tp'), may hold values from 1 to 6
- out_weight: bfloat16 [2048, 2880], P('tp'), may hold values from -0.5 to 0.5
- mlp_gain: float32 [2880], replicated, may hold values from 0.5 to 1.5
- router_weight: bfloat16 [2880, 16], replicated, may hold values from -0.21875 to 0.21875
- expert_gate: bfloat16 [16, 2880, 2880], P('req', None, 'tp'), may hold values from -0.4375 to 0.4375
- expert_up: bfloat16 [16, 2880, 2880], P('req', None, 'tp'), may hold values from -0.4375 to 0.4375
- expert_down: bfloat16 [16, 2880, 2880], P('req', 'tp'), may hold values from -0.109375 to 0.109375
- next_gain: float32 [2880], replicated, may hold values from 0.5 to 1.5
- next_q_weight: bfloat16 [2880, 2048], P(None, 'tp'), may hold values from -0.109375 to 0.109375
- following_key_value_weight: bfloat16 [2880, 2, 512], P(None, None, 'tp'), may hold values from -0.109375 to 0.109375
Outputs:
- layer_out: bfloat16 [4, 64, 2880], P(None, 'req')
- next_query: bfloat16 [4, 64, 2048], P(None, 'req', 'tp')
- next_keyval: bfloat16 [4, 64, 2, 512], P(None, 'req', None, 'tp')
Inputs may be any that keep to these rules, and one draw needn't show every extreme that they name: `lengths`: some group's prompt holds exactly 2048 positions. `routes`: a row names 4 different experts; in the rows of one device at one step no expert is named more than 4 times, a bound that some block reaches.
All inputs are finite; a program needn't handle non-finite values.
Results may differ from a plain program's by a relative error of at most 0.029.
Values may be sent and summed in bfloat16 or wider, within the bound.
A program may use at most 128 MiB of HBM per device.

v0:
```python
import jax
import jax.numpy as jnp
from jax import lax
from jax.sharding import PartitionSpec as P

HEAD = 64
EXPERTS = 16
THETA = 150000.0
EPS = 1e-05
NEG = -1e30
BF = jnp.bfloat16
F32 = jnp.float32


def rope(vectors, positions):
    half = HEAD // 2
    powers = jnp.arange(half, dtype=F32) * (2.0 / HEAD)
    angles = positions.astype(F32)[..., None, None] * jnp.power(THETA, -powers)
    cos, sin = (jnp.cos(angles), jnp.sin(angles))
    lower, upper = (vectors[..., :half], vectors[..., half:])
    return jnp.concatenate([lower * cos - upper * sin, lower * sin + upper * cos], axis=-1)


def rms(rows, gain):
    return rows * lax.rsqrt(jnp.mean(rows * rows, axis=-1, keepdims=True) + EPS) * gain


def lineage_tables(parents):
    steps, groups, beams = parents.shape
    ident = jnp.broadcast_to(jnp.arange(beams, dtype=jnp.int32), (groups, beams))
    first = []
    tokens = [[None] * steps for _ in range(steps)]
    for t in range(steps):
        walker = ident
        for s in range(t, -1, -1):
            tokens[s][t] = walker
            hot = walker[..., None] == jnp.arange(beams, dtype=jnp.int32)
            walker = jnp.sum(jnp.where(hot, parents[s][:, None, :], 0), axis=-1)
        first.append(walker)
        for s in range(t + 1, steps):
            tokens[s][t] = jnp.full_like(ident, -1)
    return (jnp.stack(first), jnp.stack([jnp.stack(row) for row in tokens]))


def local(
    layer_in,
    query_in,
    key_in,
    value_in,
    prompt_keys,
    prompt_values,
    gen_keys,
    gen_values,
    lengths,
    parents,
    routes,
    sinks,
    out_weight,
    mlp_gain,
    router_weight,
    expert_gate,
    expert_up,
    expert_down,
    next_gain,
    next_q_weight,
    next_kv_weight,
):
    req_count = lax.axis_size("req")
    me = lax.axis_index("req")
    T, B, q_width = query_in.shape
    kv_width = key_in.shape[2]
    K = kv_width // HEAD
    R = q_width // kv_width
    J = parents.shape[2]
    span = req_count // J
    beam = me // span
    start = me % span * B
    groups = [[c + span * j for j in range(J)] for c in range(span)]
    if span == 1:
        groups = None
    lens = lax.dynamic_slice_in_dim(lengths, start, B)
    pars = lax.dynamic_slice_in_dim(parents, start, B, axis=1)
    S = prompt_keys.shape[1]
    G = gen_keys.shape[1]
    pos = lens[None, :] + G + jnp.arange(T, dtype=jnp.int32)[:, None]
    q = rope(query_in.astype(F32).reshape(T, B, K * R, HEAD), pos).astype(BF).reshape(T, B, q_width)
    k = rope(key_in.astype(F32).reshape(T, B, K, HEAD), pos).astype(BF).reshape(T, B, kv_width)
    q_all = lax.all_gather(q, "req", axis_index_groups=groups)
    first, tokens = lineage_tables(pars)
    prompt_ok = (beam * S + jnp.arange(S, dtype=jnp.int32))[None, :] < lens[:, None]
    mask = jnp.concatenate(
        [
            jnp.broadcast_to(prompt_ok[:, None, None, :], (B, J, T, S)),
            jnp.broadcast_to((first == beam).transpose(1, 2, 0)[..., None], (B, J, T, G)),
            (tokens == beam).transpose(2, 3, 1, 0),
        ],
        axis=-1,
    )
    keys = jnp.concatenate([prompt_keys, gen_keys, k.transpose(1, 0, 2)], axis=1)
    values = jnp.concatenate([prompt_values, gen_values, value_in.transpose(1, 0, 2)], axis=1)
    keys = keys.reshape(B, S + G + T, K, HEAD)
    values = values.reshape(B, S + G + T, K, HEAD)
    qs = q_all.reshape(J, T, B, K, R, HEAD)
    scores = jnp.einsum("jtbkrd,bskd->bkjtrs", qs, keys, preferred_element_type=F32) * 0.125
    usable = mask[:, None, :, :, None, :]
    scores = jnp.where(usable, scores, NEG)
    high = jnp.max(scores, axis=-1)
    weights = jnp.where(usable, jnp.exp(scores - high[..., None]), 0.0)
    total = jnp.sum(weights, axis=-1)
    part = jnp.einsum("bkjtrs,bskd->jtbkrd", weights.astype(BF), values, preferred_element_type=F32)
    high = high.transpose(2, 3, 0, 1, 4)
    total = total.transpose(2, 3, 0, 1, 4)
    part = (part / jnp.maximum(total, 1e-30)[..., None]).astype(BF)
    stats = jnp.stack([high, total], axis=1)
    part = lax.all_to_all(part, "req", 0, 0, axis_index_groups=groups)
    stats = lax.all_to_all(stats, "req", 0, 0, axis_index_groups=groups)
    high, total = (stats[:, 0], stats[:, 1])
    sink = sinks.reshape(K, R)
    peak = jnp.maximum(jnp.max(high, axis=0), sink)
    share = total * jnp.exp(high - peak)
    bottom = jnp.sum(share, axis=0) + jnp.exp(sink - peak)
    attended = jnp.sum(part.astype(F32) * (share / bottom)[..., None], axis=0)
    attended = attended.astype(BF).reshape(T * B, q_width)
    projected = jnp.dot(attended, out_weight, preferred_element_type=F32)
    x1 = layer_in.reshape(T * B, -1).astype(F32) + lax.psum(projected.astype(BF), "tp").astype(F32)
    h2 = rms(x1, mlp_gain).astype(BF)
    logits = jnp.dot(h2, router_weight, preferred_element_type=F32)
    hot = jnp.sum(
        (routes.reshape(T * B, -1, 1) == jnp.arange(EXPERTS, dtype=jnp.int32)).astype(F32), axis=1
    )
    masked = jnp.where(hot > 0, logits, NEG)
    raw = jnp.where(hot > 0, jnp.exp(masked - jnp.max(masked, axis=-1, keepdims=True)), 0.0)
    gates = raw / jnp.sum(raw, axis=-1, keepdims=True)
    h2_all = lax.all_gather(h2, "req", tiled=True)
    gates_all = lax.all_gather(gates, "req", tiled=True)
    slabs = expert_gate.shape[0]
    split = slabs * req_count // EXPERTS
    moe = 0.0
    for s in range(slabs):
        expert = (me * slabs + s) // split
        weight = lax.dynamic_slice_in_dim(gates_all, expert, 1, axis=1)
        gate = jnp.minimum(jnp.dot(h2_all, expert_gate[s], preferred_element_type=F32), 7.0)
        up = jnp.clip(jnp.dot(h2_all, expert_up[s], preferred_element_type=F32), -7.0, 7.0)
        hidden = ((up + 1.0) * gate * jax.nn.sigmoid(1.702 * gate) * weight).astype(BF)
        moe = moe + jnp.dot(hidden, expert_down[s], preferred_element_type=F32)
    moe = lax.psum_scatter(moe.astype(BF), "req", scatter_dimension=0, tiled=True)
    moe = lax.psum(moe, "tp").astype(F32)
    x2 = x1 + moe
    h3 = rms(x2, next_gain).astype(BF)
    next_query = jnp.dot(h3, next_q_weight, preferred_element_type=F32).astype(BF)
    next_kv = jnp.einsum("nd,dcf->ncf", h3, next_kv_weight, preferred_element_type=F32).astype(BF)
    return (
        x2.astype(BF).reshape(T, B, -1),
        next_query.reshape(T, B, q_width),
        next_kv.reshape(T, B, 2, kv_width),
    )


def solution(mesh):
    placed = (
        P(None, "req", None),
        P(None, "req", "tp"),
        P(None, "req", "tp"),
        P(None, "req", "tp"),
        P("req", None, "tp"),
        P("req", None, "tp"),
        P("req", None, "tp"),
        P("req", None, "tp"),
        P(),
        P(),
        P(None, "req", None),
        P("tp"),
        P("tp", None),
        P(),
        P(),
        P("req", None, "tp"),
        P("req", None, "tp"),
        P("req", "tp", None),
        P(),
        P(None, "tp"),
        P(None, None, "tp"),
    )
    return jax.shard_map(
        local,
        mesh=mesh,
        in_specs=placed,
        out_specs=(P(None, "req", None), P(None, "req", "tp"), P(None, "req", None, "tp")),
        check_vma=False,
    )
```

profile of v0, /device:TPU:0, one launch (start us, length us, event | category | flops | bytes accessed | tf_op | source)
XLA Modules:
  0.0 316.0 jit_solution(11140793845565401066)
XLA Ops:
  7.2 0.8 broadcast_add_fusion
  8.0 0.8 broadcast_compare_fusion.1
  8.8 0.7 slice_bitcast_fusion.4
  9.5 0.2 select_reduce_fusion.3
  9.8 0.4 select_reduce_fusion.6
  10.1 0.5 select_reduce_fusion.8
  10.7 0.7 select_reduce_fusion.9
  11.5 0.3 copy.117
  11.8 0.1 multiply_cosine_fusion
  12.0 0.8 reshape.192
  12.8 0.1 fusion.120
  12.9 0.1 pad_maximum_fusion.4
  13.0 0.1 convert_element_type.88
  13.1 0.9 reshape.190
  14.0 0.1 subtract_convert_fusion
  14.1 0.1 pad_maximum_fusion.3
  14.2 0.1 convert_element_type.87
  14.3 34.5 %all_gather.9 = bf16[8,4,8,512]{3,2,1,0:T(8,128)(2,1)} all-gather(bf16[1,4,8,512]{3,2,1,0:T(8,128)(2,1)S(1)} %convert_element_type.87), channel_id=1, replica_groups=mesh['req'=8,'tp'=4] {'req'}, dimensions={0}, use_global_device_ids=true | all-gather | bytes 294912 | tf_op jit(solution)/shard_map/all_gather | solution.py:88
  48.8 1.3 reshape.181
  50.1 2.0 pad_maximum_fusion.1
  52.1 2.2 copy.122
  54.4 0.1 broadcast_in_dim.144
  54.5 0.1 pad_add_fusion
  54.6 2.0 fusion.24
  56.7 1.6 copy-done.1
  58.3 1.3 fusion.25
  59.6 0.8 pad_maximum_fusion.2
  60.4 1.3 copy.125
  61.7 0.9 reshape.201
  62.6 5.5 %all-to-all-start.1 = ((f32[8,1,512]{2,1,0:T(1,128)}), f32[8,1,512]{2,1,0:T(1,128)S(1)}, u32[]{:S(2)}, u32[]{:S(2)}) async-start(f32[8,1,512]{2,1,0:T(1,128)} %reshape.201), calls=%async_computation.1 | async-start | bytes 32768 | tf_op jit(solution)/shard_map/all_to_all | solution.py:116
  68.1 2.0 pad_maximum_fusion
  70.1 2.2 copy.115
  72.4 3.9 %divide_convert_fusion = bf16[8,4,8,2,4,64]{5,0,4,1,3,2:T(8,128)(2,1)} fusion(bf16[8,324,2,64,1,1]{1,3,5,4,2,0:T(8,128)(2,1)} %bitcast.191, f32[8,2,8,4,4,324]{5,2,4,3,1,0:T(8,128)} %copy-done.1, f32[8,2,8,4,4]{2,4,3,1,0:T(4,128)S(1)} %copy-done.6, pred[8,8,4,324]{3,1,2,0:T(8,128)(4,1)} %copy-done.7, f32[8,4,8,2,4]{0,4,1,3,2:T(4,128)S(1)} %bitcast_maximum_fusion), kind=kOutput, calls=%fused_computation.55 | convolution fusion | flops 88514560 | bytes 3679232 | tf_op jit(solution)/shard_map/bkjtrs,bskd->jtbkrd/dot_general | solution.py:110
  76.3 1.2 copy.157
  77.6 1.1 reshape.199
  78.7 6.0 %all-to-all-start = ((bf16[8,2,8192]{2,1,0:T(2,128)(2,1)}), bf16[8,2,8192]{2,1,0:T(2,128)(2,1)}, u32[]{:S(2)}, u32[]{:S(2)}) async-start(bf16[8,2,8192]{2,1,0:T(2,128)(2,1)} %reshape.199), calls=%async_computation | async-start | bytes 524288 | tf_op jit(solution)/shard_map/all_to_all | solution.py:115
  84.7 0.5 broadcast.189
  85.2 0.7 reduce.1
  85.9 0.3 reshape.202
  86.4 0.1 fusion.119
  86.6 0.5 copy.127
  87.1 5.9 %all-to-all-done = bf16[8,2,8192]{2,1,0:T(2,128)(2,1)} async-done(((bf16[8,2,8192]{2,1,0:T(2,128)(2,1)}), bf16[8,2,8192]{2,1,0:T(2,128)(2,1)}, u32[]{:S(2)}, u32[]{:S(2)}) %all-to-all-start) | async-done | bytes 262176 | tf_op jit(solution)/shard_map/all_to_all | solution.py:115
  93.0 2.1 reshape.200
  95.1 1.7 multiply_reduce_fusion
  96.9 0.1 convert_element_type.93
  97.0 1.6 convolution_convert_fusion
  98.7 29.9 %all-reduce.3.cloned.1.call-done = bf16[32,2880]{1,0:T(8,128)(2,1)} async-done(((bf16[32,2880]{1,0:T(8,128)(2,1)}), bf16[32,2880]{1,0:T(8,128)(2,1)}) %all-reduce.3.cloned.1.call-update) | async-done | bytes 184336 | tf_op jit(solution)/shard_map/psum | solution.py:125
  128.6 1.1 multiply_reduce_fusion.2
  129.8 1.7 multiply_convert_fusion.1
  131.6 0.1 eq.163
  131.7 1.1 fusion.121
  132.8 30.8 %all-gather = f32[8,32,16]{1,2,0:T(8,128)S(1)} all-gather(f32[1,32,16]{1,2,0:T(8,128)S(1)} %divide_bitcast_fusion), channel_id=1, replica_groups=mesh['req'=8,'tp'=4] {'req'}, dimensions={0}, use_global_device_ids=true | all-gather | bytes 18432 | tf_op jit(solution)/shard_map/all_gather | solution.py:135
  163.8 11.5 %all-gather.3.cloned.1.call-done = bf16[256,2880]{1,0:T(8,128)(2,1)} async-done(((bf16[32,2880]{1,0:T(8,128)(2,1)}), bf16[256,2880]{1,0:T(8,128)(2,1)}) %all-gather.3.cloned.1.call-update) | async-done | bytes 1474576 | tf_op jit(solution)/shard_map/all_gather | solution.py:134
  175.3 5.0 %fusion.48 = f32[256,720]{0,1:T(8,128)} fusion(bf16[256,2880]{1,0:T(8,128)(2,1)} %all-gather.3.cloned.1.call-done, bf16[2,2880,720]{1,2,0:T(8,128)(2,1)} %param.36), kind=kOutput, calls=%fused_computation.38 | convolution fusion | flops 1061867520 | bytes 6483968 | tf_op jit(solution)/shard_map/dot_general | solution.py:142
  180.3 4.4 %fusion.42 = f32[256,720]{0,1:T(8,128)} fusion(bf16[256,2880]{1,0:T(8,128)(2,1)S(1)} %copy-done.13, bf16[2,2880,720]{1,2,0:T(8,128)(2,1)} %param.36), kind=kOutput, calls=%fused_computation.36 | convolution fusion | flops 1061867520 | bytes 6451200 | tf_op jit(solution)/shard_map/dot_general | solution.py:142
  184.7 10.7 %fusion = f32[256,2880]{1,0:T(8,128)} fusion(bf16[2,720,2880]{2,1,0:T(8,128)(2,1)} %param.38, f32[256,720]{0,1:T(8,128)} %fusion.48, bf16[256,2880]{1,0:T(8,128)(2,1)} %all-gather.3.cloned.1.call-done, bf16[2,2880,720]{1,2,0:T(8,128)(2,1)} %param.37, f32[256]{0:T(256)S(1)} %bitcast.205), kind=kOutput, calls=%fused_computation | convolution fusion | flops 2125209600 | bytes 13673472 | tf_op jit(solution)/shard_map/dot_general | solution.py:145
  195.3 11.1 %fusion.21 = bf16[256,2880]{1,0:T(8,128)(2,1)} fusion(f32[256,2880]{1,0:T(8,128)} %fusion, bf16[2,720,2880]{2,1,0:T(8,128)(2,1)} %param.38, f32[256,720]{0,1:T(8,128)} %fusion.42, bf16[256,2880]{1,0:T(8,128)(2,1)} %all-gather.3.cloned.1.call-done, bf16[2,2880,720]{1,2,0:T(8,128)(2,1)} %param.37, f32[256]{0:T(256)S(1)} %bitcast.204), kind=kOutput, calls=%fused_computation.19 | convolution fusion | flops 2126684160 | bytes 15213568 | tf_op jit(solution)/shard_map/dot_general | solution.py:145
  206.5 63.7 %reduce-scatter.2.cloned.1.call-done = bf16[32,2880]{1,0:T(8,128)(2,1)} async-done(((bf16[256,2880]{1,0:T(8,128)(2,1)}), bf16[32,2880]{1,0:T(8,128)(2,1)}) %reduce-scatter.2.cloned.1.call-update) | async-done | bytes 184336 | tf_op jit(solution)/shard_map/reduce_scatter | solution.py:146
  270.2 32.6 %all-reduce.5.cloned.1.call-done = bf16[32,2880]{1,0:T(8,128)(2,1)} async-done(((bf16[32,2880]{1,0:T(8,128)(2,1)}), bf16[32,2880]{1,0:T(8,128)(2,1)}) %all-reduce.5.cloned.1.call-update) | async-done | bytes 184336 | tf_op jit(solution)/shard_map/psum | solution.py:147
  302.9 1.3 multiply_reduce_fusion.1
  304.2 1.7 multiply_convert_fusion
  305.9 1.7 fusion.85
  307.6 1.2 fusion.81
  308.8 0.6 copy.133
  (72 shorter events, 1.1 us)
Async XLA Ops:
  7.2 89.8 %copy-start = (bf16[512,2880]{0,1:T(8,128)(2,1)S(1)}, bf16[512,2880]{0,1:T(8,128)(2,1)}, u32[]{:S(2)}) copy-start(bf16[512,2880]{0,1:T(8,128)(2,1)} %param.33) | copy-start | bytes 8847364
  54.6 5.0 %copy-start.7 = (pred[8,8,4,324]{3,1,2,0:T(8,128)(4,1)}, pred[8,8,4,324]{3,1,2,0:T(8,128)(4,1)S(1)}, u32[]{:S(2)}) copy-start(pred[8,8,4,324]{3,1,2,0:T(8,128)(4,1)S(1)} %pad_add_fusion) | copy-start | bytes 248836
  56.7 1.7 copy-start.1
  56.7 2.9 copy-start.5
  56.7 11.4 %copy-start.11 = (bf16[4,8,128]{2,1,0:T(8,128)(2,1)S(1)}, bf16[4,8,128]{2,1,0:T(8,128)(2,1)}, u32[]{:S(2)}) copy-start(bf16[4,8,128]{2,1,0:T(8,128)(2,1)} %param.24) | copy-start | bytes 24580
  60.4 12.0 %copy-start.6 = (f32[8,2,8,4,4]{2,4,3,1,0:T(4,128)S(1)}, f32[8,2,8,4,4]{2,4,3,1,0:T(4,128)}, u32[]{:S(2)}) copy-start(f32[8,2,8,4,4]{2,4,3,1,0:T(4,128)} %copy-done.5) | copy-start | bytes 24580
  62.6 16.1 %all-to-all-start.1 = ((f32[8,1,512]{2,1,0:T(1,128)}), f32[8,1,512]{2,1,0:T(1,128)S(1)}, u32[]{:S(2)}, u32[]{:S(2)}) async-start(f32[8,1,512]{2,1,0:T(1,128)} %reshape.201), calls=%async_computation.1 | async-start | bytes 32768 | tf_op jit(solution)/shard_map/all_to_all | solution.py:116
  72.4 3.9 %copy-start.14 = (f32[8]{0:T(128)S(1)}, f32[8]{0:T(128)}, u32[]{:S(2)}) copy-start(f32[8]{0:T(128)} %param.32) | copy-start | bytes 100
  78.7 14.3 %all-to-all-start = ((bf16[8,2,8192]{2,1,0:T(2,128)(2,1)}), bf16[8,2,8192]{2,1,0:T(2,128)(2,1)}, u32[]{:S(2)}, u32[]{:S(2)}) async-start(bf16[8,2,8192]{2,1,0:T(2,128)(2,1)} %reshape.199), calls=%async_computation | async-start | bytes 524288 | tf_op jit(solution)/shard_map/all_to_all | solution.py:115
  84.7 44.0 %all-reduce.3.cloned.1.call-start = ((), (), s32[]{:S(2)}) async-start(), calls=%async_computation.3 | async-start | bytes 376832 | tf_op jit(solution)/shard_map/psum | solution.py:125
  86.4 42.3 %copy-start.2 = (bf16[4,8,2880]{2,1,0:T(8,128)(2,1)S(1)}, bf16[4,8,2880]{2,1,0:T(8,128)(2,1)}, u32[]{:S(2)}) copy-start(bf16[4,8,2880]{2,1,0:T(8,128)(2,1)} %param.21) | copy-start | bytes 552964
  86.6 43.2 %copy-start.10 = (f32[2880]{0:T(1024)S(1)}, f32[2880]{0:T(1024)}, u32[]{:S(2)}) copy-start(f32[2880]{0:T(1024)} %param.34) | copy-start | bytes 34564
  87.1 44.5 %copy-start.12 = (s32[4,8,4]{1,2,0:T(4,128)S(1)}, s32[4,8,4]{1,2,0:T(4,128)}, u32[]{:S(2)}) copy-start(s32[4,8,4]{1,2,0:T(4,128)} %param.31) | copy-start | bytes 1540
  87.1 44.6 %copy-start.8 = (bf16[2880,16]{0,1:T(8,128)(2,1)S(1)}, bf16[2880,16]{0,1:T(8,128)(2,1)}, u32[]{:S(2)}) copy-start(bf16[2880,16]{0,1:T(8,128)(2,1)} %param.35) | copy-start | bytes 276484
  98.6 76.6 %all-gather.3.cloned.1.call-start = ((), (), s32[]{:S(2)}) async-start(), calls=%async_computation.4 | async-start | bytes 1695744 | tf_op jit(solution)/shard_map/all_gather | solution.py:134
  131.5 138.7 %reduce-scatter.2.cloned.1.call-start = ((), (), s32[]{:S(2)}) async-start(), calls=%async_computation.5 | async-start | bytes 1695744 | tf_op jit(solution)/shard_map/reduce_scatter | solution.py:146
  175.3 5.0 %copy-start.13 = (bf16[256,2880]{1,0:T(8,128)(2,1)S(1)}, bf16[256,2880]{1,0:T(8,128)(2,1)}, u32[]{:S(2)}) copy-start(bf16[256,2880]{1,0:T(8,128)(2,1)} %all-gather.3.cloned.1.call-done) | copy-start | bytes 4423684
  195.3 107.5 %copy-start.3 = (bf16[32,2880]{1,0:T(8,128)(2,1)S(1)}, bf16[32,2880]{1,0:T(8,128)(2,1)}, u32[]{:S(2)}) copy-start(bf16[32,2880]{1,0:T(8,128)(2,1)} %all-reduce.3.cloned.1.call-done) | copy-start | bytes 552964
  195.3 108.8 %copy-start.9 = (f32[2880]{0:T(1024)S(1)}, f32[2880]{0:T(1024)}, u32[]{:S(2)}) copy-start(f32[2880]{0:T(1024)} %param.39) | copy-start | bytes 34564
  206.4 96.4 %all-reduce.5.cloned.1.call-start = ((), (), s32[]{:S(2)}) async-start(), calls=%async_computation.6 | async-start | bytes 376832 | tf_op jit(solution)/shard_map/psum | solution.py:147
  302.9 4.8 %copy-start.4 = (bf16[2880,512]{1,0:T(8,128)(2,1)S(1)}, bf16[2880,512]{1,0:T(8,128)(2,1)}, u32[]{:S(2)}) copy-start(bf16[2880,512]{1,0:T(8,128)(2,1)} %param.40) | copy-start | bytes 8847364
Sparse Core Ops, SparseCore 0:
  98.8 29.8 all-reduce.2
  131.6 43.5 all-gather.2
  206.6 63.5 reduce-scatter.1
  272.4 30.4 all-reduce.4
where the time goes:
time: 317 us; the launch traced here: 316 us
  waiting for transfers between devices  144 us (45%)
  blocking collectives  65.4 us (21%)
  matrix products  42.8 us (14%)
  local copies, waits for them, and re-layouts  19.6 us (6%)
  other arithmetic  18.8 us (6%)
  between operations  14.2 us (4%)
  starting transfers between devices  11.6 us (4%)
    reduce_scatter x1, waiting for transfers between devices, local(): lax.psum_scatter(moe.astype(BF), 'req', scatter_dimension=0, tiled=True)  63.7 us
    all_gather x1, blocking collectives, local(): q_all = lax.all_gather(q, 'req', axis_index_groups=groups)  34.5 us
    psum x1, waiting for transfers between devices, local(): moe = lax.psum(moe, 'tp').astype(F32)  32.6 us
    all_gather x1, blocking collectives, local(): gates_all = lax.all_gather(gates, 'req', tiled=True)  30.8 us
    psum x1, waiting for transfers between devices, local(): lax.psum(projected.astype(BF), 'tp').astype(F32)  29.9 us
    dot_general x2, matrix products, local(): moe = moe + jnp.dot(hidden, expert_down[s], preferred_element_type=F32)  21.7 us
    all_gather x1, waiting for transfers between devices, local(): h2_all = lax.all_gather(h2, 'req', tiled=True)  11.5 us
    dot_general x2, matrix products, local(): jnp.dot(h2_all, expert_gate[s], preferred_element_type=F32)  9.4 us
  transfers between devices with their start and end apart: 6, of which 5 were waited for; matrix products, arithmetic and copies ran while one was open for 5% of the time, Pallas kernels for 0%

commit v1 on v0

--- a/solution.py
+++ b/solution.py
@@ -1,3 +1,4 @@
+import functools
 import jax
 import jax.numpy as jnp
 from jax import lax
@@ -10,6 +11,43 @@
 NEG = -1e30
 BF = jnp.bfloat16
 F32 = jnp.float32
+
+
+def hold_flows_all(base_x, dim_k):
+    base_x = jnp.moveaxis(base_x, 0, dim_k)
+    found_now = base_x.shape
+    next_value = base_x.reshape(
+        *found_now[:dim_k], found_now[dim_k] * found_now[dim_k + 1], *found_now[dim_k + 2 :]
+    )
+    return next_value
+
+
+def surface_supply_all(view, peer_axis, axis_no):
+    n = jax.lax.axis_size(peer_axis)
+    ledger = []
+    for it in tuple(range(n)):
+        ledger.append((it, (it + 1) % n))
+    arrivals = []
+    for m, h in ledger:
+        arrivals.append((h, m))
+    block_out, right_arr = ([], [])
+    for dev in [*range(n - 1)]:
+        if dev % 2 == 0:
+            block_out.append(
+                jax.lax.ppermute(block_out[-1] if block_out else view, peer_axis, ledger)
+            )
+        else:
+            right_arr.append(
+                jax.lax.ppermute(right_arr[-1] if right_arr else view, peer_axis, arrivals)
+            )
+    left_arr = jnp.stack([*block_out[::-1], view, *right_arr], axis=0)
+    carry_in = jax.lax.axis_index(peer_axis) - len(block_out)
+    left_arr = left_arr[(jnp.arange(n) - carry_in) % n]
+    part_next = hold_flows_all(left_arr, axis_no)
+    return part_next
+
+
+handle_shifts_all = functools.partial(surface_supply_all, peer_axis="req", axis_no=0)
 
 
 def rope(vectors, positions):
@@ -132,7 +170,7 @@
     raw = jnp.where(hot > 0, jnp.exp(masked - jnp.max(masked, axis=-1, keepdims=True)), 0.0)
     gates = raw / jnp.sum(raw, axis=-1, keepdims=True)
     h2_all = lax.all_gather(h2, "req", tiled=True)
-    gates_all = lax.all_gather(gates, "req", tiled=True)
+    gates_all = handle_shifts_all(gates)
     slabs = expert_gate.shape[0]
     split = slabs * req_count // EXPERTS
     moe = 0.0

time: 317 us -> 317 us (level)
  blocking collectives: 65.4 us -> 34.5 us
  starting transfers between devices: 11.6 us -> 27.6 us
  waiting for transfers between devices: 144 us -> 158 us
    all_gather x1 -> x0, blocking collectives: 30.8 us -> none  [local(): gates_all = lax.all_gather(gates, 'req', tiled=True)]
    ppermute x0 -> x7, starting transfers between devices: none -> 16 us  [the longest x3 14.4 us: surface_supply_all(): jax.lax.ppermute(right_arr[-1] if right_arr else view, peer_axis, arrivals)]
    ppermute x0 -> x7, waiting for transfers between devices: none -> 9.54 us  [the longest x4 9.53 us: surface_supply_all(): jax.lax.ppermute(block_out[-1] if block_out else view, peer_axis, ledger)]
    all_gather x1, waiting for transfers between devices: 11.5 us -> 16.4 us  [local(): h2_all = lax.all_gather(h2, 'req', tiled=True)]
    unnamed x38 -> x44, local copies, waits for them, and re-layouts: 6.82 us -> 6.76 us
  transfers between devices with their start and end apart: 6 -> 13, of which waited for: 5 -> 9; matrix products, arithmetic and copies ran while one was open for 5% -> 5% of each run, Pallas kernels for 0% -> 0%
where the time goes in v1:
time: 317 us; the launch traced here: 316 us
  waiting for transfers between devices  158 us (50%)
  matrix products  42.8 us (14%)
  blocking collectives  34.5 us (11%)
  starting transfers between devices  27.6 us (9%)
  local copies, waits for them, and re-layouts  20.1 us (6%)
  other arithmetic  18.8 us (6%)
  between operations  14.3 us (5%)
    reduce_scatter x1, waiting for transfers between devices, local(): lax.psum_scatter(moe.astype(BF), 'req', scatter_dimension=0, tiled=True)  63.6 us
    all_gather x1, blocking collectives, local(): q_all = lax.all_gather(q, 'req', axis_index_groups=groups)  34.5 us
    psum x1, waiting for transfers between devices, local(): moe = lax.psum(moe, 'tp').astype(F32)  32.7 us
    psum x1, waiting for transfers between devices, local(): lax.psum(projected.astype(BF), 'tp').astype(F32)  29.9 us
    dot_general x2, matrix products, local(): moe = moe + jnp.dot(hidden, expert_down[s], preferred_element_type=F32)  21.7 us
    all_gather x1, waiting for transfers between devices, local(): h2_all = lax.all_gather(h2, 'req', tiled=True)  16.4 us
    ppermute x3, starting transfers between devices, surface_supply_all(): jax.lax.ppermute(right_arr[-1] if right_arr else view, peer_axis, arrivals)  14.4 us
    ppermute x4, waiting for transfers between devices, surface_supply_all(): jax.lax.ppermute(block_out[-1] if block_out else view, peer_axis, ledger)  9.53 us
  transfers between devices with their start and end apart: 13, of which 9 were waited for; matrix products, arithmetic and copies ran while one was open for 5% of the time, Pallas kernels for 0%

profile of v1, /device:TPU:0, one launch (start us, length us, event | category | flops | bytes accessed | tf_op | source)
XLA Modules:
  0.0 316.2 jit_solution(2496233003103804721)
XLA Ops:
  7.2 0.8 broadcast_add_fusion
  8.0 0.8 broadcast_compare_fusion.1
  8.8 0.7 slice_bitcast_fusion.4
  9.5 0.2 select_reduce_fusion.3
  9.8 0.4 select_reduce_fusion.6
  10.1 0.5 select_reduce_fusion.8
  10.7 0.7 select_reduce_fusion.9
  11.5 0.3 copy.117
  11.8 0.1 multiply_cosine_fusion
  12.0 0.8 reshape.245
  13.1 0.9 reshape.243
  14.2 0.1 convert_element_type.87
  14.3 34.5 %all_gather.6 = bf16[8,4,8,512]{3,2,1,0:T(8,128)(2,1)} all-gather(bf16[1,4,8,512]{3,2,1,0:T(8,128)(2,1)S(1)} %convert_element_type.87), channel_id=1, replica_groups=mesh['req'=8,'tp'=4] {'req'}, dimensions={0}, use_global_device_ids=true | all-gather | bytes 294912 | tf_op jit(solution)/shard_map/all_gather | solution.py:126
  48.8 1.3 reshape.233
  50.1 2.0 pad_maximum_fusion.1
  52.1 2.2 copy.122
  54.5 0.1 pad_add_fusion
  54.6 2.0 fusion.24
  56.7 1.6 copy-done.1
  58.3 1.3 fusion.25
  59.6 0.8 pad_maximum_fusion.2
  60.4 1.3 copy.125
  61.7 0.9 reshape.260
  62.6 5.5 %all-to-all-start.1 = ((f32[8,1,512]{2,1,0:T(1,128)}), f32[8,1,512]{2,1,0:T(1,128)S(1)}, u32[]{:S(2)}, u32[]{:S(2)}) async-start(f32[8,1,512]{2,1,0:T(1,128)} %reshape.260), calls=%async_computation.1 | async-start | bytes 32768 | tf_op jit(solution)/shard_map/all_to_all | solution.py:154
  68.1 2.0 pad_maximum_fusion
  70.1 2.2 copy.115
  72.4 3.9 %divide_convert_fusion = bf16[8,4,8,2,4,64]{5,0,4,1,3,2:T(8,128)(2,1)} fusion(bf16[8,324,2,64,1,1]{1,3,5,4,2,0:T(8,128)(2,1)} %bitcast.207, f32[8,2,8,4,4,324]{5,2,4,3,1,0:T(8,128)} %copy-done.1, f32[8,2,8,4,4]{2,4,3,1,0:T(4,128)S(1)} %copy-done.6, pred[8,8,4,324]{3,1,2,0:T(8,128)(4,1)} %copy-done.7, f32[8,4,8,2,4]{0,4,1,3,2:T(4,128)S(1)} %bitcast_maximum_fusion), kind=kOutput, calls=%fused_computation.56 | convolution fusion | flops 88514560 | bytes 3679232 | tf_op jit(solution)/shard_map/bkjtrs,bskd->jtbkrd/dot_general | solution.py:148
  76.4 1.2 copy.157
  77.7 1.1 reshape.258
  78.8 6.0 %all-to-all-start = ((bf16[8,2,8192]{2,1,0:T(2,128)(2,1)}), bf16[8,2,8192]{2,1,0:T(2,128)(2,1)}, u32[]{:S(2)}, u32[]{:S(2)}) async-start(bf16[8,2,8192]{2,1,0:T(2,128)(2,1)} %reshape.258), calls=%async_computation | async-start | bytes 524288 | tf_op jit(solution)/shard_map/all_to_all | solution.py:153
  84.8 0.5 broadcast.258
  85.3 0.7 reduce.1
  86.0 0.3 reshape.261
  86.7 0.5 copy.127
  87.2 5.9 %all-to-all-done = bf16[8,2,8192]{2,1,0:T(2,128)(2,1)} async-done(((bf16[8,2,8192]{2,1,0:T(2,128)(2,1)}), bf16[8,2,8192]{2,1,0:T(2,128)(2,1)}, u32[]{:S(2)}, u32[]{:S(2)}) %all-to-all-start) | async-done | bytes 262176 | tf_op jit(solution)/shard_map/all_to_all | solution.py:153
  93.1 2.1 reshape.259
  95.2 1.7 multiply_reduce_fusion
  97.0 0.1 convert_element_type.93
  97.1 1.6 convolution_convert_fusion
  98.8 29.9 %all-reduce.3.cloned.1.call-done = bf16[32,2880]{1,0:T(8,128)(2,1)} async-done(((bf16[32,2880]{1,0:T(8,128)(2,1)}), bf16[32,2880]{1,0:T(8,128)(2,1)}) %all-reduce.3.cloned.1.call-update) | async-done | bytes 184336 | tf_op jit(solution)/shard_map/psum | solution.py:163
  128.8 1.1 multiply_reduce_fusion.2
  129.9 1.7 multiply_convert_fusion.1
  131.7 1.1 fusion.124
  132.8 1.5 collective-permute-start
  134.3 4.9 %collective-permute-done = f32[32,16]{0,1:T(8,128)S(1)} collective-permute-done((f32[32,16]{0,1:T(8,128)S(1)}, f32[32,16]{0,1:T(8,128)S(1)}, u32[]{:S(2)}, u32[]{:S(2)}) %collective-permute-start) | collective-permute-done | bytes 2080 | tf_op jit(solution)/shard_map/ppermute | solution.py:37
  139.2 4.7 %collective-permute-start.4 = (f32[32,16]{0,1:T(8,128)S(1)}, f32[32,16]{0,1:T(8,128)S(1)}, u32[]{:S(2)}, u32[]{:S(2)}) collective-permute-start(f32[32,16]{0,1:T(8,128)S(1)} %fusion.107), channel_id=1, source_target_pairs={{4,0},{8,4},{12,8},{16,12},{20,16},{24,20},{28,24},{0,28},{5,1},{9... | collective-permute-start | bytes 6152 | tf_op jit(solution)/shard_map/ppermute | solution.py:41
  143.9 1.7 collective-permute-done.1
  145.7 4.8 %collective-permute-start.5 = (f32[32,16]{0,1:T(8,128)S(1)}, f32[32,16]{0,1:T(8,128)S(1)}, u32[]{:S(2)}, u32[]{:S(2)}) collective-permute-start(f32[32,16]{0,1:T(8,128)S(1)} %collective-permute-done.4), channel_id=1, source_target_pairs={{4,0},{8,4},{12,8},{16,12},{20,16},{24,20},{28,24},{0,28},{5,1},{9... | collective-permute-start | bytes 6152 | tf_op jit(solution)/shard_map/ppermute | solution.py:41
  150.5 1.5 collective-permute-done.2
  152.0 4.9 %collective-permute-start.6 = (f32[32,16]{0,1:T(8,128)S(1)}, f32[32,16]{0,1:T(8,128)S(1)}, u32[]{:S(2)}, u32[]{:S(2)}) collective-permute-start(f32[32,16]{0,1:T(8,128)S(1)} %collective-permute-done.5), channel_id=1, source_target_pairs={{4,0},{8,4},{12,8},{16,12},{20,16},{24,20},{28,24},{0,28},{5,1},{9... | collective-permute-start | bytes 6152 | tf_op jit(solution)/shard_map/ppermute | solution.py:41
  157.0 1.4 collective-permute-done.3
  158.4 0.6 gather_fusion
  159.1 16.4 %all-gather.2.cloned.1.call-done = bf16[256,2880]{1,0:T(8,128)(2,1)} async-done(((bf16[32,2880]{1,0:T(8,128)(2,1)}), bf16[256,2880]{1,0:T(8,128)(2,1)}) %all-gather.2.cloned.1.call-update) | async-done | bytes 1474576 | tf_op jit(solution)/shard_map/all_gather | solution.py:172
  175.5 5.0 %fusion.48 = f32[256,720]{0,1:T(8,128)} fusion(bf16[256,2880]{1,0:T(8,128)(2,1)} %all-gather.2.cloned.1.call-done, bf16[2,2880,720]{1,2,0:T(8,128)(2,1)} %param.36), kind=kOutput, calls=%fused_computation.39 | convolution fusion | flops 1061867520 | bytes 6483968 | tf_op jit(solution)/shard_map/dot_general | solution.py:180
  180.5 4.4 %fusion.42 = f32[256,720]{0,1:T(8,128)} fusion(bf16[256,2880]{1,0:T(8,128)(2,1)S(1)} %copy-done.13, bf16[2,2880,720]{1,2,0:T(8,128)(2,1)} %param.36), kind=kOutput, calls=%fused_computation.37 | convolution fusion | flops 1061867520 | bytes 6451200 | tf_op jit(solution)/shard_map/dot_general | solution.py:180
  184.9 10.7 %fusion = f32[256,2880]{1,0:T(8,128)} fusion(bf16[2,720,2880]{2,1,0:T(8,128)(2,1)} %param.38, f32[256,720]{0,1:T(8,128)} %fusion.48, bf16[256,2880]{1,0:T(8,128)(2,1)} %all-gather.2.cloned.1.call-done, bf16[2,2880,720]{1,2,0:T(8,128)(2,1)} %param.37, f32[256]{0:T(256)S(1)} %bitcast.221), kind=kOutput, calls=%fused_computation.1 | convolution fusion | flops 2125209600 | bytes 13673472 | tf_op jit(solution)/shard_map/dot_general | solution.py:183
  195.6 11.1 %fusion.21 = bf16[256,2880]{1,0:T(8,128)(2,1)} fusion(f32[256,2880]{1,0:T(8,128)} %fusion, bf16[2,720,2880]{2,1,0:T(8,128)(2,1)} %param.38, f32[256,720]{0,1:T(8,128)} %fusion.42, bf16[256,2880]{1,0:T(8,128)(2,1)} %all-gather.2.cloned.1.call-done, bf16[2,2880,720]{1,2,0:T(8,128)(2,1)} %param.37, f32[256]{0:T(256)S(1)} %bitcast.220), kind=kOutput, calls=%fused_computation.20 | convolution fusion | flops 2126684160 | bytes 15213568 | tf_op jit(solution)/shard_map/dot_general | solution.py:183
  206.7 63.6 %reduce-scatter.2.cloned.1.call-done = bf16[32,2880]{1,0:T(8,128)(2,1)} async-done(((bf16[256,2880]{1,0:T(8,128)(2,1)}), bf16[32,2880]{1,0:T(8,128)(2,1)}) %reduce-scatter.2.cloned.1.call-update) | async-done | bytes 184336 | tf_op jit(solution)/shard_map/reduce_scatter | solution.py:184
  270.4 32.7 %all-reduce.5.cloned.1.call-done = bf16[32,2880]{1,0:T(8,128)(2,1)} async-done(((bf16[32,2880]{1,0:T(8,128)(2,1)}), bf16[32,2880]{1,0:T(8,128)(2,1)}) %all-reduce.5.cloned.1.call-update) | async-done | bytes 184336 | tf_op jit(solution)/shard_map/psum | solution.py:185
  303.1 1.3 multiply_reduce_fusion.1
  304.3 1.7 multiply_convert_fusion
  306.1 1.7 fusion.85
  307.8 1.2 fusion.81
  309.0 0.6 copy.133
  (96 shorter events, 1.9 us)
Async XLA Ops:
  7.2 89.9 %copy-start = (bf16[512,2880]{0,1:T(8,128)(2,1)S(1)}, bf16[512,2880]{0,1:T(8,128)(2,1)}, u32[]{:S(2)}) copy-start(bf16[512,2880]{0,1:T(8,128)(2,1)} %param.33) | copy-start | bytes 8847364
  54.6 5.0 %copy-start.7 = (pred[8,8,4,324]{3,1,2,0:T(8,128)(4,1)}, pred[8,8,4,324]{3,1,2,0:T(8,128)(4,1)S(1)}, u32[]{:S(2)}) copy-start(pred[8,8,4,324]{3,1,2,0:T(8,128)(4,1)S(1)} %pad_add_fusion) | copy-start | bytes 248836
  56.7 1.7 copy-start.1
  56.7 2.9 copy-start.5
  56.7 11.4 %copy-start.11 = (bf16[4,8,128]{2,1,0:T(8,128)(2,1)S(1)}, bf16[4,8,128]{2,1,0:T(8,128)(2,1)}, u32[]{:S(2)}) copy-start(bf16[4,8,128]{2,1,0:T(8,128)(2,1)} %param.24) | copy-start | bytes 24580
  60.4 12.0 %copy-start.6 = (f32[8,2,8,4,4]{2,4,3,1,0:T(4,128)S(1)}, f32[8,2,8,4,4]{2,4,3,1,0:T(4,128)}, u32[]{:S(2)}) copy-start(f32[8,2,8,4,4]{2,4,3,1,0:T(4,128)} %copy-done.5) | copy-start | bytes 24580
  62.6 16.2 %all-to-all-start.1 = ((f32[8,1,512]{2,1,0:T(1,128)}), f32[8,1,512]{2,1,0:T(1,128)S(1)}, u32[]{:S(2)}, u32[]{:S(2)}) async-start(f32[8,1,512]{2,1,0:T(1,128)} %reshape.260), calls=%async_computation.1 | async-start | bytes 32768 | tf_op jit(solution)/shard_map/all_to_all | solution.py:154
  72.4 3.9 %copy-start.14 = (f32[8]{0:T(128)S(1)}, f32[8]{0:T(128)}, u32[]{:S(2)}) copy-start(f32[8]{0:T(128)} %param.32) | copy-start | bytes 100
  72.4 4.0 %copy-start.12 = (s32[4,8,4]{1,2,0:T(4,128)S(1)}, s32[4,8,4]{1,2,0:T(4,128)}, u32[]{:S(2)}) copy-start(s32[4,8,4]{1,2,0:T(4,128)} %param.31) | copy-start | bytes 1540
  78.8 14.3 %all-to-all-start = ((bf16[8,2,8192]{2,1,0:T(2,128)(2,1)}), bf16[8,2,8192]{2,1,0:T(2,128)(2,1)}, u32[]{:S(2)}, u32[]{:S(2)}) async-start(bf16[8,2,8192]{2,1,0:T(2,128)(2,1)} %reshape.258), calls=%async_computation | async-start | bytes 524288 | tf_op jit(solution)/shard_map/all_to_all | solution.py:153
  84.8 44.0 %all-reduce.3.cloned.1.call-start = ((), (), s32[]{:S(2)}) async-start(), calls=%async_computation.3 | async-start | bytes 376832 | tf_op jit(solution)/shard_map/psum | solution.py:163
  86.5 42.3 %copy-start.2 = (bf16[4,8,2880]{2,1,0:T(8,128)(2,1)S(1)}, bf16[4,8,2880]{2,1,0:T(8,128)(2,1)}, u32[]{:S(2)}) copy-start(bf16[4,8,2880]{2,1,0:T(8,128)(2,1)} %param.21) | copy-start | bytes 552964
  86.7 43.2 %copy-start.10 = (f32[2880]{0:T(1024)S(1)}, f32[2880]{0:T(1024)}, u32[]{:S(2)}) copy-start(f32[2880]{0:T(1024)} %param.34) | copy-start | bytes 34564
  87.2 44.5 %copy-start.8 = (bf16[2880,16]{0,1:T(8,128)(2,1)S(1)}, bf16[2880,16]{0,1:T(8,128)(2,1)}, u32[]{:S(2)}) copy-start(bf16[2880,16]{0,1:T(8,128)(2,1)} %param.35) | copy-start | bytes 276484
  98.8 76.8 %all-gather.2.cloned.1.call-start = ((), (), s32[]{:S(2)}) async-start(), calls=%async_computation.4 | async-start | bytes 1695744 | tf_op jit(solution)/shard_map/all_gather | solution.py:172
  131.6 138.8 %reduce-scatter.2.cloned.1.call-start = ((), (), s32[]{:S(2)}) async-start(), calls=%async_computation.5 | async-start | bytes 1695744 | tf_op jit(solution)/shard_map/reduce_scatter | solution.py:184
  132.8 6.4 %collective-permute-start = (f32[32,16]{0,1:T(8,128)S(1)}, f32[32,16]{0,1:T(8,128)S(1)}, u32[]{:S(2)}, u32[]{:S(2)}) collective-permute-start(f32[32,16]{0,1:T(8,128)S(1)} %fusion.107), channel_id=1, source_target_pairs={{0,4},{4,8},{8,12},{12,16},{16,20},{20,24},{24,28},{28,0},{1,5},{5... | collective-permute-start | bytes 6152 | tf_op jit(solution)/shard_map/ppermute | solution.py:37
  139.2 6.4 %collective-permute-start.1 = (f32[32,16]{0,1:T(8,128)S(1)}, f32[32,16]{0,1:T(8,128)S(1)}, u32[]{:S(2)}, u32[]{:S(2)}) collective-permute-start(f32[32,16]{0,1:T(8,128)S(1)} %collective-permute-done), channel_id=1, source_target_pairs={{0,4},{4,8},{8,12},{12,16},{16,20},{20,24},{24,28},{28,0},{1,5},{5... | collective-permute-start | bytes 6152 | tf_op jit(solution)/shard_map/ppermute | solution.py:37
  139.2 6.5 %collective-permute-start.4 = (f32[32,16]{0,1:T(8,128)S(1)}, f32[32,16]{0,1:T(8,128)S(1)}, u32[]{:S(2)}, u32[]{:S(2)}) collective-permute-start(f32[32,16]{0,1:T(8,128)S(1)} %fusion.107), channel_id=1, source_target_pairs={{4,0},{8,4},{12,8},{16,12},{20,16},{24,20},{28,24},{0,28},{5,1},{9... | collective-permute-start | bytes 6152 | tf_op jit(solution)/shard_map/ppermute | solution.py:41
  145.7 6.3 %collective-permute-start.2 = (f32[32,16]{0,1:T(8,128)S(1)}, f32[32,16]{0,1:T(8,128)S(1)}, u32[]{:S(2)}, u32[]{:S(2)}) collective-permute-start(f32[32,16]{0,1:T(8,128)S(1)} %collective-permute-done.1), channel_id=1, source_target_pairs={{0,4},{4,8},{8,12},{12,16},{16,20},{20,24},{24,28},{28,0},{1,5},{5... | collective-permute-start | bytes 6152 | tf_op jit(solution)/shard_map/ppermute | solution.py:37
  145.7 6.3 %collective-permute-start.5 = (f32[32,16]{0,1:T(8,128)S(1)}, f32[32,16]{0,1:T(8,128)S(1)}, u32[]{:S(2)}, u32[]{:S(2)}) collective-permute-start(f32[32,16]{0,1:T(8,128)S(1)} %collective-permute-done.4), channel_id=1, source_target_pairs={{4,0},{8,4},{12,8},{16,12},{20,16},{24,20},{28,24},{0,28},{5,1},{9... | collective-permute-start | bytes 6152 | tf_op jit(solution)/shard_map/ppermute | solution.py:41
  152.0 6.3 %collective-permute-start.3 = (f32[32,16]{0,1:T(8,128)S(1)}, f32[32,16]{0,1:T(8,128)S(1)}, u32[]{:S(2)}, u32[]{:S(2)}) collective-permute-start(f32[32,16]{0,1:T(8,128)S(1)} %collective-permute-done.2), channel_id=1, source_target_pairs={{0,4},{4,8},{8,12},{12,16},{16,20},{20,24},{24,28},{28,0},{1,5},{5... | collective-permute-start | bytes 6152 | tf_op jit(solution)/shard_map/ppermute | solution.py:37
  152.0 6.4 %collective-permute-start.6 = (f32[32,16]{0,1:T(8,128)S(1)}, f32[32,16]{0,1:T(8,128)S(1)}, u32[]{:S(2)}, u32[]{:S(2)}) collective-permute-start(f32[32,16]{0,1:T(8,128)S(1)} %collective-permute-done.5), channel_id=1, source_target_pairs={{4,0},{8,4},{12,8},{16,12},{20,16},{24,20},{28,24},{0,28},{5,1},{9... | collective-permute-start | bytes 6152 | tf_op jit(solution)/shard_map/ppermute | solution.py:41
  175.5 5.0 %copy-start.13 = (bf16[256,2880]{1,0:T(8,128)(2,1)S(1)}, bf16[256,2880]{1,0:T(8,128)(2,1)}, u32[]{:S(2)}) copy-start(bf16[256,2880]{1,0:T(8,128)(2,1)} %all-gather.2.cloned.1.call-done) | copy-start | bytes 4423684
  195.6 107.5 %copy-start.3 = (bf16[32,2880]{1,0:T(8,128)(2,1)S(1)}, bf16[32,2880]{1,0:T(8,128)(2,1)}, u32[]{:S(2)}) copy-start(bf16[32,2880]{1,0:T(8,128)(2,1)} %all-reduce.3.cloned.1.call-done) | copy-start | bytes 552964
  195.6 108.8 %copy-start.9 = (f32[2880]{0:T(1024)S(1)}, f32[2880]{0:T(1024)}, u32[]{:S(2)}) copy-start(f32[2880]{0:T(1024)} %param.39) | copy-start | bytes 34564
  206.7 96.4 %all-reduce.5.cloned.1.call-start = ((), (), s32[]{:S(2)}) async-start(), calls=%async_computation.6 | async-start | bytes 376832 | tf_op jit(solution)/shard_map/psum | solution.py:185
  303.0 4.8 %copy-start.4 = (bf16[2880,512]{1,0:T(8,128)(2,1)S(1)}, bf16[2880,512]{1,0:T(8,128)(2,1)}, u32[]{:S(2)}) copy-start(bf16[2880,512]{1,0:T(8,128)(2,1)} %param.40) | copy-start | bytes 8847364
Sparse Core Ops, SparseCore 0:
  98.9 29.8 all-reduce.2
  131.7 43.7 all-gather.1
  206.8 63.5 reduce-scatter.1
  272.5 30.4 all-reduce.4
